TPU v7x, 128 devices: a whole 4x4x4 slice. The times are simulated.
128 devices in a mesh: ctx: 16 (over y, x), tp: 8 (over z, core).
Axes of the slice: x: 4, y: 4, z: 4, core: 2. Of those that a mesh axis runs over, the one named last changes fastest.
Arguments:
- query_rows: bfloat16 [8192, 8192], P('ctx', 'tp'), may hold values from -6 to 6
- key_rows: bfloat16 [8192, 8192], P('ctx', 'tp'), may hold values from -6 to 6
- value_rows: bfloat16 [8192, 8192], P('ctx', 'tp'), may hold values from -6 to 6
- positions: int32 [16, 512], replicated, may hold values from -1 to 255, as said below
- filters: float32 [8192, 4096], P(('tp', 'ctx')), may hold values from -6 to 6
- bias_term: float32 [8192], P(('tp', 'ctx')), may hold values from -4 to 4
- grad_out: bfloat16 [4096, 8192], P(('ctx', 'tp')), may hold values from -6 to 6
Outputs:
- output: bfloat16 [4096, 8192], P('ctx', 'tp')
- grad_query: bfloat16 [4096, 8192], P('ctx', 'tp')
- grad_key: bfloat16 [4096, 8192], P('ctx', 'tp')
- grad_value: bfloat16 [4096, 8192], P('ctx', 'tp')
- grad_filters: float32 [8192, 4096], P(('tp', 'ctx'))
Inputs may be any that keep to these rules, and one draw needn't show every extreme that they name: Entries j * 32 to (j + 1) * 32 - 1 of row i list the positions within context shard j of the rows that loader buffer i holds for shard j, or -1 for an unused row; live rows come first in such a slot and carry consecutive positions (one run of a segment). Over all buffers every position of every shard appears exactly once, and for every shard some buffer fills its whole slot of 32 rows.
All inputs are finite; a program needn't handle non-finite values.
Results may differ from a plain program's by a relative error of at most 0.0058.
Values may be sent and summed in bfloat16 or wider, within the bound.
A program may use at most 128 MiB of HBM per device.

v0:
```python
import math

import jax
import jax.numpy as jnp
import numpy as np
from jax import lax
from jax.experimental import pallas as pl
from jax.experimental.pallas import tpu as pltpu
from jax.sharding import PartitionSpec as P

MESH = pl.DeviceIdType.MESH
BF = jnp.bfloat16
F32 = jnp.float32


def split_bf16(table):
    high = table.astype(jnp.bfloat16)
    low = (table - high.astype(np.float64)).astype(jnp.bfloat16)
    return high, low


def make_tables(shards, tokens):
    length = 2 * shards * tokens
    r = np.arange(tokens)
    inner = 2.0 * math.pi * ((r[:, None] * r[None, :]) % tokens) / tokens
    cos, sin = np.cos(inner), np.sin(inner)
    forward = np.block([[cos, -sin], [sin, cos]])
    backward = np.block([[cos, sin], [-sin, cos]])
    k = np.arange(shards + 1)
    twist = 2.0 * math.pi * (k[:, None] * r[None, :]) / length
    return (
        split_bf16(forward),
        split_bf16(backward),
        np.cos(twist).astype(np.float32),
        np.sin(twist).astype(np.float32),
    )


def real_dft_padded(xs):
    half = len(xs)
    if half == 1:
        return [(xs[0], None), (xs[0], None)]
    even = real_dft_padded(xs[0::2])
    odd = real_dft_padded(xs[1::2])
    out = [None] * (half + 1)
    out[0] = (even[0][0] + odd[0][0], None)
    out[half] = (even[0][0] - odd[0][0], None)
    mid = half // 2
    for k in range(1, mid):
        angle = math.pi * k / half
        c, s = math.cos(angle), math.sin(angle)
        o_re, o_im = odd[k]
        t_re = o_re * c + o_im * s
        t_im = o_im * c - o_re * s
        e_re, e_im = even[k]
        out[k] = (e_re + t_re, e_im + t_im)
        out[half - k] = (e_re - t_re, t_im - e_im)
    out[mid] = (even[mid][0], -odd[mid][0])
    return out


def real_inverse_half(bins):
    half = len(bins) - 1
    if half == 1:
        return [bins[0][0] + bins[1][0]]
    mid = half // 2
    even = [None] * (mid + 1)
    odd = [None] * (mid + 1)
    even[0] = (bins[0][0] + bins[half][0], None)
    odd[0] = (bins[0][0] - bins[half][0], None)
    for k in range(1, mid):
        angle = math.pi * k / half
        c, s = math.cos(angle), math.sin(angle)
        a_re, a_im = bins[k]
        b_re, b_im = bins[half - k]
        even[k] = (a_re + b_re, a_im - b_im)
        d_re, d_im = a_re - b_re, a_im + b_im
        odd[k] = (d_re * c - d_im * s, d_im * c + d_re * s)
    m_re, m_im = bins[mid]
    even[mid] = (m_re + m_re, None)
    odd[mid] = (-(m_im + m_im), None)
    y_even = real_inverse_half(even)
    y_odd = real_inverse_half(odd)
    out = [None] * half
    out[0::2] = y_even
    out[1::2] = y_odd
    return out


def kernel_body(
    sizes,
    q_hbm, k_hbm, v_hbm, g_hbm, f_hbm, wf_hi_hbm, wf_lo_hbm, wi_hi_hbm, wi_lo_hbm,
    slot_ref, bias_ref, cos_ref, sin_ref,
    out_ref, gq_ref, gk_ref, gv_ref, gf_ref,
    rq, rk, rv, gtok, f_buf, wf_hi, wf_lo, wi_hi, wi_lo,
    hot, q_seq, k_seq, v_seq, sig_t, gc_t, sig_in, gc_in,
    l_hi, l_lo, spec_f, spec_s, spec_g, z_buf,
    conv_o, gs_o, conv_t, gs_t,
    recv_sem, send_sem, local_sem,
):
    n_ctx, n_tp, tok, slot, chan = sizes
    side = 4
    width = n_ctx * chan
    me = lax.axis_index("ctx")
    my_tp = lax.axis_index("tp")
    my_y, my_x = me // side, me % side
    factor = 1.0 / math.sqrt(n_ctx * tok)
    inv_len = 1.0 / (2 * n_ctx * tok)
    bins = n_ctx + 1

    def partner(o):
        return ((my_y + o // side) % side) * side + (my_x + o % side) % side

    def each_partner(fn):
        lax.fori_loop(1, n_ctx, lambda o, c: (fn(partner(o)), c)[1], 0)

    loads = [
        pltpu.make_async_copy(src, dst, local_sem.at[n])
        for n, (src, dst) in enumerate(
            ((f_hbm, f_buf), (wf_hi_hbm, wf_hi), (wf_lo_hbm, wf_lo), (wi_hi_hbm, wi_hi), (wi_lo_hbm, wi_lo))
        )
    ]
    for copy in loads:
        copy.start()

    barrier = pltpu.get_barrier_semaphore()
    each_partner(
        lambda d: pl.semaphore_signal(barrier, inc=1, device_id=(d, my_tp), device_id_type=MESH)
    )
    lax.fori_loop(
        1,
        n_tp,
        lambda o, c: (
            pl.semaphore_signal(
                barrier, inc=1, device_id=(me, (my_tp + o) % n_tp), device_id_type=MESH
            ),
            c,
        )[1],
        0,
    )
    pl.semaphore_wait(barrier, n_ctx + n_tp - 2)

    def send_rows(src, dst, n):
        def one(d):
            pltpu.make_async_remote_copy(
                src_ref=src.at[pl.ds(pl.multiple_of(d * slot, slot), slot), :],
                dst_ref=dst.at[pl.ds(pl.multiple_of(me * slot, slot), slot), :],
                send_sem=send_sem.at[n],
                recv_sem=recv_sem.at[n],
                device_id=(d, my_tp),
                device_id_type=MESH,
            ).start()

        own = pl.ds(pl.multiple_of(me * slot, slot), slot)
        pltpu.make_async_copy(src.at[own, :], dst.at[own, :], recv_sem.at[n]).start()
        each_partner(one)

    send_rows(k_hbm, rk, 0)
    send_rows(v_hbm, rv, 1)

    def send_grad(o, carry):
        d = (my_tp + o) % n_tp
        pltpu.make_async_remote_copy(
            src_ref=g_hbm.at[:, pl.ds(pl.multiple_of(d * width, width), width)],
            dst_ref=gtok.at[pl.ds(pl.multiple_of(my_tp * slot, slot), slot), :],
            send_sem=send_sem.at[3],
            recv_sem=recv_sem.at[3],
            device_id=(me, d),
            device_id_type=MESH,
        ).start()
        return carry

    pltpu.make_async_copy(
        g_hbm.at[:, pl.ds(pl.multiple_of(my_tp * width, width), width)],
        gtok.at[pl.ds(pl.multiple_of(my_tp * slot, slot), slot), :],
        recv_sem.at[3],
    ).start()
    lax.fori_loop(1, n_tp, send_grad, 0)
    send_rows(q_hbm, rq, 2)

    hot[...] = jnp.where(
        slot_ref[...] == lax.broadcasted_iota(jnp.int32, hot.shape, 0), 1.0, 0.0
    ).astype(BF)

    row_step, lane_step = 16, 128
    halves = tok // lane_step
    pieces = (chan // row_step) * halves

    def place(it):
        rows = pl.multiple_of((it // halves) * row_step, row_step)
        lanes = pl.multiple_of((it % halves) * lane_step, lane_step)
        return rows, lanes

    def put_split(row, lane, value):
        high = value.astype(BF)
        at = (pl.ds(pl.multiple_of(row, row_step), row_step), pl.ds(pl.multiple_of(lane, lane_step), lane_step))
        l_hi[at] = high
        l_lo[at] = (value - high.astype(F32)).astype(BF)

    def forward_outer(load):
        def step(it, carry):
            rows, lanes = place(it)
            spectrum = real_dft_padded([load(j, rows, lanes) for j in range(n_ctx)])
            for k in range(bins):
                re, im = spectrum[k]
                if k == 0:
                    put_split(rows, lanes, re)
                    put_split(rows, tok + lanes, jnp.zeros_like(re))
                    continue
                c = cos_ref[k : k + 1, pl.ds(lanes, lane_step)]
                s = sin_ref[k : k + 1, pl.ds(lanes, lane_step)]
                if im is None:
                    t_re, t_im = re * c, -(re * s)
                else:
                    t_re, t_im = re * c + im * s, im * c - re * s
                put_split(k * chan + rows, lanes, t_re)
                put_split(k * chan + rows, tok + lanes, t_im)
            return carry

        lax.fori_loop(0, pieces, step, 0)

    total_rows = bins * chan
    block_rows = total_rows // 4

    def inner(high, low, dest):
        def step(m, carry):
            at = pl.ds(pl.multiple_of(m * block_rows, row_step), block_rows)
            a, b = l_hi[at, :], l_lo[at, :]
            dest[at, :] = (
                jnp.dot(a, high[...], preferred_element_type=F32)
                + jnp.dot(a, low[...], preferred_element_type=F32)
                + jnp.dot(b, high[...], preferred_element_type=F32)
            )
            return carry

        lax.fori_loop(0, 4, step, 0)

    def multiply(one, two, conjugate_one):
        def step(m, carry):
            row = m * row_step
            at = pl.ds(pl.multiple_of(row, row_step), row_step)
            for lane in range(0, tok, lane_step):
                re_at, im_at = slice(lane, lane + lane_step), slice(tok + lane, tok + lane + lane_step)
                a, b = one[at, re_at], one[at, im_at]
                c, d = two[at, re_at], two[at, im_at]
                if conjugate_one:
                    re, im = a * c + b * d, a * d - b * c
                else:
                    re, im = a * c - b * d, a * d + b * c
                put_split(row, lane, re)
                put_split(row, tok + lane, im)
            return carry

        lax.fori_loop(0, total_rows // row_step, step, 0)

    def inverse_outer(store):
        def step(it, carry):
            rows, lanes = place(it)
            spectrum = []
            for k in range(bins):
                at = pl.ds(pl.multiple_of(k * chan + rows, row_step), row_step)
                re = z_buf[at, pl.ds(lanes, lane_step)]
                if k == 0:
                    spectrum.append((re, None))
                    continue
                im = z_buf[at, pl.ds(pl.multiple_of(tok + lanes, lane_step), lane_step)]
                c = cos_ref[k : k + 1, pl.ds(lanes, lane_step)]
                s = sin_ref[k : k + 1, pl.ds(lanes, lane_step)]
                if k == n_ctx:
                    spectrum.append((re * c - im * s, None))
                else:
                    spectrum.append((re * c - im * s, im * c + re * s))
            for j, y in enumerate(real_inverse_half(spectrum)):
                store(j, rows, lanes, y * (factor * inv_len))
            return carry

        lax.fori_loop(0, pieces, step, 0)

    for copy in loads:
        copy.wait()
    forward_outer(
        lambda j, rows, lanes: f_buf[
            pl.ds(rows, row_step), pl.ds(pl.multiple_of(j * tok + lanes, lane_step), lane_step)
        ]
    )
    inner(wf_hi, wf_lo, spec_f)

    def wait_all(buf, n):
        pltpu.make_async_copy(buf, buf, recv_sem.at[n]).wait()

    def settled(rows_ref, cols):
        return jnp.dot(hot[...], rows_ref[:, cols], preferred_element_type=F32)

    group = side * chan

    def send_channels(src, dst, n, y):
        def one(dx, carry):
            d = y * side + (my_x + dx) % side
            at = pl.ds(pl.multiple_of(d * chan, chan), chan)
            pl.when(d != me)(
                lambda: pltpu.make_async_remote_copy(
                    src_ref=src.at[at, :],
                    dst_ref=dst.at[me],
                    send_sem=send_sem.at[n],
                    recv_sem=recv_sem.at[n],
                    device_id=(d, my_tp),
                    device_id_type=MESH,
                ).start()
            )
            return carry

        lax.fori_loop(0, side, one, 0)

    def send_own_channels(src, dst, n):
        at = pl.ds(pl.multiple_of(me * chan, chan), chan)
        pltpu.make_async_copy(src.at[at, :], dst.at[me], recv_sem.at[n]).start()

    wait_all(rk, 0)
    wait_all(rv, 1)

    def signal_step(i, carry):
        y = (my_y + i) % side
        cols = pl.ds(pl.multiple_of(y * group, group), group)
        key = settled(rk, cols)
        value = settled(rv, cols)
        k_seq[:, cols] = key.astype(BF)
        v_seq[:, cols] = value.astype(BF)
        sig_t[cols, :] = (key * value).T.astype(BF)
        send_channels(sig_t, sig_in, 4, y)
        return carry

    lax.fori_loop(0, side, signal_step, 0)
    send_own_channels(sig_t, sig_in, 4)

    wait_all(rq, 2)
    wait_all(gtok, 3)

    def grad_step(i, carry):
        y = (my_y + i) % side
        cols = pl.ds(pl.multiple_of(y * group, group), group)
        query = settled(rq, cols)
        q_seq[:, cols] = query.astype(BF)
        gc_t[cols, :] = (query * gtok[:, cols].astype(F32)).T.astype(BF)
        send_channels(gc_t, gc_in, 5, y)
        return carry

    lax.fori_loop(0, side, grad_step, 0)
    send_own_channels(gc_t, gc_in, 5)

    def send_tokens(src, dst, n):
        at = pl.ds(pl.multiple_of(me * chan, chan), chan)

        def one(d):
            pltpu.make_async_remote_copy(
                src_ref=src.at[d],
                dst_ref=dst.at[at, :],
                send_sem=send_sem.at[n],
                recv_sem=recv_sem.at[n],
                device_id=(d, my_tp),
                device_id_type=MESH,
            ).start()

        pltpu.make_async_copy(src.at[me], dst.at[at, :], recv_sem.at[n]).start()
        each_partner(one)

    def piece(buf, j, rows, lanes):
        return buf[j, pl.ds(rows, row_step), pl.ds(lanes, lane_step)].astype(F32)

    def store_with_bias(direct, dest):
        def store(j, rows, lanes, y):
            bias = bias_ref[pl.ds(rows, row_step), :]
            dest[j, pl.ds(rows, row_step), pl.ds(lanes, lane_step)] = (
                bias * piece(direct, j, rows, lanes) + y
            ).astype(BF)

        return store

    wait_all(sig_in, 4)
    forward_outer(lambda j, rows, lanes: piece(sig_in, j, rows, lanes))
    inner(wf_hi, wf_lo, spec_s)
    multiply(spec_f, spec_s, False)
    inner(wi_hi, wi_lo, z_buf)
    inverse_outer(store_with_bias(sig_in, conv_o))
    send_tokens(conv_o, conv_t, 6)

    wait_all(gc_in, 5)
    forward_outer(lambda j, rows, lanes: piece(gc_in, j, rows, lanes))
    inner(wf_hi, wf_lo, spec_g)
    multiply(spec_f, spec_g, True)
    inner(wi_hi, wi_lo, z_buf)
    inverse_outer(store_with_bias(gc_in, gs_o))
    send_tokens(gs_o, gs_t, 7)

    multiply(spec_s, spec_g, True)
    inner(wi_hi, wi_lo, z_buf)

    def store_filter(j, rows, lanes, y):
        gf_ref[pl.ds(rows, row_step), pl.ds(pl.multiple_of(j * tok + lanes, lane_step), lane_step)] = y

    inverse_outer(store_filter)

    wait_all(conv_t, 6)

    def output_step(i, carry):
        cols = pl.ds(pl.multiple_of(i * group, group), group)
        conv = conv_t[cols, :].astype(F32).T
        out_ref[:, cols] = (q_seq[:, cols].astype(F32) * conv).astype(BF)
        gq_ref[:, cols] = (gtok[:, cols].astype(F32) * conv).astype(BF)
        return carry

    lax.fori_loop(0, side, output_step, 0)

    wait_all(gs_t, 7)

    def gradient_step(i, carry):
        cols = pl.ds(pl.multiple_of(i * group, group), group)
        grad = gs_t[cols, :].astype(F32).T
        gk_ref[:, cols] = (grad * v_seq[:, cols].astype(F32)).astype(BF)
        gv_ref[:, cols] = (grad * k_seq[:, cols].astype(F32)).astype(BF)
        return carry

    lax.fori_loop(0, side, gradient_step, 0)

    def wait_sent(buf, n):
        pltpu.make_async_copy(buf, buf, send_sem.at[n]).wait()

    rows_sent = pl.ds(0, (n_ctx - 1) * slot)
    wait_sent(rk.at[rows_sent, :], 0)
    wait_sent(rv.at[rows_sent, :], 1)
    wait_sent(rq.at[rows_sent, :], 2)
    wait_sent(gtok.at[pl.ds(0, (n_tp - 1) * slot), :], 3)
    parts_sent = pl.ds(0, n_ctx - 1)
    wait_sent(sig_in.at[parts_sent], 4)
    wait_sent(gc_in.at[parts_sent], 5)
    wait_sent(conv_o.at[parts_sent], 6)
    wait_sent(gs_o.at[parts_sent], 7)


def solution(mesh):
    n_ctx, n_tp = mesh.shape["ctx"], mesh.shape["tp"]

    def per_device(query_rows, key_rows, value_rows, positions, filters, bias_term, grad_out):
        width = query_rows.shape[1]
        slot = query_rows.shape[0] // n_ctx
        tok = grad_out.shape[0] * n_tp
        chan = filters.shape[0]
        (wf_hi, wf_lo), (wi_hi, wi_lo), cos, sin = make_tables(n_ctx, tok)
        own = lax.dynamic_slice_in_dim(positions, lax.axis_index("ctx") * slot, slot, 1)
        own = own.reshape(1, n_ctx * slot)
        bins = n_ctx + 1
        vm = pltpu.VMEM
        rows_bf = vm((n_ctx * slot, width), BF)
        seq = vm((tok, width), BF)
        seq_t = vm((width, tok), BF)
        parts = vm((n_ctx, chan, tok), BF)
        spec = vm((bins * chan, 2 * tok), F32)
        half_spec = vm((bins * chan, 2 * tok), BF)
        table = vm((2 * tok, 2 * tok), BF)
        any_spec = pl.BlockSpec(memory_space=pl.ANY)
        vmem_spec = pl.BlockSpec(memory_space=pltpu.VMEM)
        seq_out = jax.ShapeDtypeStruct((tok, width), BF)

        def body(*refs):
            kernel_body((n_ctx, n_tp, tok, slot, chan), *refs)

        return pl.pallas_call(
            body,
            out_shape=(seq_out, seq_out, seq_out, seq_out, jax.ShapeDtypeStruct(filters.shape, F32)),
            in_specs=[any_spec] * 9 + [vmem_spec] * 4,
            out_specs=(vmem_spec,) * 5,
            scratch_shapes=[
                rows_bf, rows_bf, rows_bf, seq, vm(filters.shape, F32), table, table, table, table,
                vm((tok, n_ctx * slot), BF), seq, seq, seq, seq_t, seq_t, parts, parts,
                half_spec, half_spec, spec, spec, spec, spec,
                parts, parts, seq_t, seq_t,
                pltpu.SemaphoreType.DMA((8,)),
                pltpu.SemaphoreType.DMA((8,)),
                pltpu.SemaphoreType.DMA((5,)),
            ],
            compiler_params=pltpu.CompilerParams(
                collective_id=0, has_side_effects=True, vmem_limit_bytes=56 * 1024 * 1024
            ),
        )(
            query_rows, key_rows, value_rows, grad_out, filters,
            wf_hi, wf_lo, wi_hi, wi_lo,
            own, bias_term.reshape(chan, 1), cos, sin,
        )

    in_specs = (
        P("ctx", "tp"),
        P("ctx", "tp"),
        P("ctx", "tp"),
        P(),
        P(("tp", "ctx"), None),
        P(("tp", "ctx")),
        P(("ctx", "tp"), None),
    )
    out_specs = (
        P("ctx", "tp"),
        P("ctx", "tp"),
        P("ctx", "tp"),
        P("ctx", "tp"),
        P(("tp", "ctx"), None),
    )
    return jax.shard_map(
        per_device, mesh=mesh, in_specs=in_specs, out_specs=out_specs, check_vma=False
    )
```

profile of v0, /device:TPU:2, one launch (start us, length us, event | category | flops | bytes accessed | tf_op | source)
XLA Modules:
  0.0 90.2 jit_solution(15643651066799668182)
XLA Ops:
  0.6 0.0 copy-start
  0.7 0.7 copy-done
  1.4 0.1 constant_dynamic-slice_fusion
  1.5 0.0 copy-start.5
  1.5 0.7 reshape.16.refs_9_
  2.1 0.0 copy-done.5
  2.1 0.7 copy.18.refs_10_
  2.8 81.6 %shard_map.164 = (bf16[256,1024]{1,0:T(8,128)(2,1)}, bf16[256,1024]{1,0:T(8,128)(2,1)}, bf16[256,1024]{1,0:T(8,128)(2,1)}, bf16[256,1024]{1,0:T(8,128)(2,1)}, f32[64,4096]{1,0:T(8,128)}) custom-call(bf16[512,1024]{1,0:T(8,128)(2,1)} %refs_0_.1, bf16[512,1024]{1,0:T(8,128)(2,1)} %refs_1_.1, bf16[512,1024]{1,0:T(8,128)(2,1)} %refs_2_.1, ...), custom_call_target="tpu_custom_call" | custom-call | tf_op jit(solution)/shard_map/pallas_call | solution.py:466
  84.4 0.0 copy-start.4
  84.4 1.9 %copy.24 = bf16[256,1024]{1,0:T(8,128)(2,1)} copy(bf16[256,1024]{1,0:T(8,128)(2,1)} %get-tuple-element.10) | data formatting | bytes 1048576
  86.4 0.0 copy-done.4
  86.4 0.0 copy-start.3
  86.4 0.0 copy-start.2
  86.4 0.8 copy.25
  87.2 0.4 copy-done.3
  87.6 0.0 copy-start.1
  87.6 0.8 copy.26
  88.4 0.0 copy-done.2
  88.4 0.8 copy.27
  89.2 0.0 copy-done.1
  89.2 1.0 %copy.28 = f32[64,4096]{1,0:T(8,128)} copy(f32[64,4096]{1,0:T(8,128)S(1)} %copy-done.1) | data formatting | bytes 2097152
Async XLA Ops:
  0.6 0.8 copy-start
  1.5 0.7 copy-start.5
  84.4 1.9 %copy-start.4 = (bf16[256,1024]{1,0:T(8,128)(2,1)S(1)}, bf16[256,1024]{1,0:T(8,128)(2,1)}, u32[]{:S(2)}) copy-start(bf16[256,1024]{1,0:T(8,128)(2,1)} %get-tuple-element.11) | copy-start | bytes 1572868
  86.4 1.2 %copy-start.3 = (bf16[256,1024]{1,0:T(8,128)(2,1)S(1)}, bf16[256,1024]{1,0:T(8,128)(2,1)}, u32[]{:S(2)}) copy-start(bf16[256,1024]{1,0:T(8,128)(2,1)} %get-tuple-element.12) | copy-start | bytes 1572868
  86.4 2.0 %copy-start.2 = (bf16[256,1024]{1,0:T(8,128)(2,1)S(1)}, bf16[256,1024]{1,0:T(8,128)(2,1)}, u32[]{:S(2)}) copy-start(bf16[256,1024]{1,0:T(8,128)(2,1)} %get-tuple-element.13) | copy-start | bytes 1572868
  87.6 1.6 %copy-start.1 = (f32[64,4096]{1,0:T(8,128)S(1)}, f32[64,4096]{1,0:T(8,128)}, u32[]{:S(2)}) copy-start(f32[64,4096]{1,0:T(8,128)} %get-tuple-element.14) | copy-start | bytes 3145732
where the time goes:
time: 91.2 us; the launch traced here: 90.2 us
  Pallas kernels  81.6 us (89%)
  local copies, waits for them, and re-layouts  7.92 us (9%)
    pallas_call x1, Pallas kernels, per_device(): pl.pallas_call(body, out_shape=(seq_out, seq_out, seq_out, seq_out, jax.S...  81.6 us
    unnamed x17, local copies, waits for them, and re-layouts  6.48 us

commit v1 on v0

--- a/solution.py
+++ b/solution.py
@@ -11,6 +11,7 @@
 MESH = pl.DeviceIdType.MESH
 BF = jnp.bfloat16
 F32 = jnp.float32
+FAR_FIRST = (10, 5, 15, 13, 7, 14, 6, 11, 9, 2, 8, 1, 12, 3, 4)
 
 
 def split_bf16(table):
@@ -91,12 +92,12 @@
     sizes,
     q_hbm, k_hbm, v_hbm, g_hbm, f_hbm, wf_hi_hbm, wf_lo_hbm, wi_hi_hbm, wi_lo_hbm,
     slot_ref, bias_ref, cos_ref, sin_ref,
-    out_ref, gq_ref, gk_ref, gv_ref, gf_ref,
+    q_out, g_out, k_out, v_out, conv_t, gs_t, f_out,
     rq, rk, rv, gtok, f_buf, wf_hi, wf_lo, wi_hi, wi_lo,
     hot, q_seq, k_seq, v_seq, sig_t, gc_t, sig_in, gc_in,
     l_hi, l_lo, spec_f, spec_s, spec_g, z_buf,
-    conv_o, gs_o, conv_t, gs_t,
-    recv_sem, send_sem, local_sem,
+    conv_o, gs_o, gf_ref,
+    recv_sem, send_sem, local_sem, out_sem,
 ):
     n_ctx, n_tp, tok, slot, chan = sizes
     side = 4
@@ -112,7 +113,8 @@
         return ((my_y + o // side) % side) * side + (my_x + o % side) % side
 
     def each_partner(fn):
-        lax.fori_loop(1, n_ctx, lambda o, c: (fn(partner(o)), c)[1], 0)
+        for o in FAR_FIRST:
+            fn(partner(o))
 
     loads = [
         pltpu.make_async_copy(src, dst, local_sem.at[n])
@@ -191,21 +193,22 @@
         lanes = pl.multiple_of((it % halves) * lane_step, lane_step)
         return rows, lanes
 
-    def put_split(row, lane, value):
+    def put_split(row, lane, value, exact):
         high = value.astype(BF)
         at = (pl.ds(pl.multiple_of(row, row_step), row_step), pl.ds(pl.multiple_of(lane, lane_step), lane_step))
         l_hi[at] = high
-        l_lo[at] = (value - high.astype(F32)).astype(BF)
-
-    def forward_outer(load):
+        if exact:
+            l_lo[at] = (value - high.astype(F32)).astype(BF)
+
+    def forward_outer(load, exact):
         def step(it, carry):
             rows, lanes = place(it)
             spectrum = real_dft_padded([load(j, rows, lanes) for j in range(n_ctx)])
             for k in range(bins):
                 re, im = spectrum[k]
                 if k == 0:
-                    put_split(rows, lanes, re)
-                    put_split(rows, tok + lanes, jnp.zeros_like(re))
+                    put_split(rows, lanes, re, exact)
+                    put_split(rows, tok + lanes, jnp.zeros_like(re), exact)
                     continue
                 c = cos_ref[k : k + 1, pl.ds(lanes, lane_step)]
                 s = sin_ref[k : k + 1, pl.ds(lanes, lane_step)]
@@ -213,8 +216,8 @@
                     t_re, t_im = re * c, -(re * s)
                 else:
                     t_re, t_im = re * c + im * s, im * c - re * s
-                put_split(k * chan + rows, lanes, t_re)
-                put_split(k * chan + rows, tok + lanes, t_im)
+                put_split(k * chan + rows, lanes, t_re, exact)
+                put_split(k * chan + rows, tok + lanes, t_im, exact)
             return carry
 
         lax.fori_loop(0, pieces, step, 0)
@@ -222,20 +225,20 @@
     total_rows = bins * chan
     block_rows = total_rows // 4
 
-    def inner(high, low, dest):
+    def inner(high, low, dest, exact):
         def step(m, carry):
             at = pl.ds(pl.multiple_of(m * block_rows, row_step), block_rows)
-            a, b = l_hi[at, :], l_lo[at, :]
-            dest[at, :] = (
-                jnp.dot(a, high[...], preferred_element_type=F32)
-                + jnp.dot(a, low[...], preferred_element_type=F32)
-                + jnp.dot(b, high[...], preferred_element_type=F32)
-            )
+            a = l_hi[at, :]
+            total = jnp.dot(a, high[...], preferred_element_type=F32)
+            total += jnp.dot(a, low[...], preferred_element_type=F32)
+            if exact:
+                total += jnp.dot(l_lo[at, :], high[...], preferred_element_type=F32)
+            dest[at, :] = total
             return carry
 
         lax.fori_loop(0, 4, step, 0)
 
-    def multiply(one, two, conjugate_one):
+    def multiply(one, two, conjugate_one, exact):
         def step(m, carry):
             row = m * row_step
             at = pl.ds(pl.multiple_of(row, row_step), row_step)
@@ -247,8 +250,8 @@
                     re, im = a * c + b * d, a * d - b * c
                 else:
                     re, im = a * c - b * d, a * d + b * c
-                put_split(row, lane, re)
-                put_split(row, tok + lane, im)
+                put_split(row, lane, re, exact)
+                put_split(row, tok + lane, im, exact)
             return carry
 
         lax.fori_loop(0, total_rows // row_step, step, 0)
@@ -281,12 +284,16 @@
     forward_outer(
         lambda j, rows, lanes: f_buf[
             pl.ds(rows, row_step), pl.ds(pl.multiple_of(j * tok + lanes, lane_step), lane_step)
-        ]
-    )
-    inner(wf_hi, wf_lo, spec_f)
+        ],
+        True,
+    )
+    inner(wf_hi, wf_lo, spec_f, True)
 
     def wait_all(buf, n):
         pltpu.make_async_copy(buf, buf, recv_sem.at[n]).wait()
+
+    def hand_out(src, dst, n):
+        pltpu.make_async_copy(src, dst, out_sem.at[n]).start()
 
     def settled(rows_ref, cols):
         return jnp.dot(hot[...], rows_ref[:, cols], preferred_element_type=F32)
@@ -331,6 +338,8 @@
 
     lax.fori_loop(0, side, signal_step, 0)
     send_own_channels(sig_t, sig_in, 4)
+    hand_out(k_seq, k_out, 0)
+    hand_out(v_seq, v_out, 1)
 
     wait_all(rq, 2)
     wait_all(gtok, 3)
@@ -346,6 +355,8 @@
 
     lax.fori_loop(0, side, grad_step, 0)
     send_own_channels(gc_t, gc_in, 5)
+    hand_out(q_seq, q_out, 2)
+    hand_out(gtok, g_out, 3)
 
     def send_tokens(src, dst, n):
         at = pl.ds(pl.multiple_of(me * chan, chan), chan)
@@ -376,50 +387,37 @@
         return store
 
     wait_all(sig_in, 4)
-    forward_outer(lambda j, rows, lanes: piece(sig_in, j, rows, lanes))
-    inner(wf_hi, wf_lo, spec_s)
-    multiply(spec_f, spec_s, False)
-    inner(wi_hi, wi_lo, z_buf)
+    forward_outer(lambda j, rows, lanes: piece(sig_in, j, rows, lanes), False)
+    inner(wf_hi, wf_lo, spec_s, False)
+    multiply(spec_f, spec_s, False, False)
+    inner(wi_hi, wi_lo, z_buf, False)
     inverse_outer(store_with_bias(sig_in, conv_o))
     send_tokens(conv_o, conv_t, 6)
 
     wait_all(gc_in, 5)
-    forward_outer(lambda j, rows, lanes: piece(gc_in, j, rows, lanes))
-    inner(wf_hi, wf_lo, spec_g)
-    multiply(spec_f, spec_g, True)
-    inner(wi_hi, wi_lo, z_buf)
+    forward_outer(lambda j, rows, lanes: piece(gc_in, j, rows, lanes), False)
+    inner(wf_hi, wf_lo, spec_g, False)
+    multiply(spec_f, spec_g, True, False)
+    inner(wi_hi, wi_lo, z_buf, False)
     inverse_outer(store_with_bias(gc_in, gs_o))
     send_tokens(gs_o, gs_t, 7)
 
-    multiply(spec_s, spec_g, True)
-    inner(wi_hi, wi_lo, z_buf)
+    multiply(spec_s, spec_g, True, True)
+    inner(wi_hi, wi_lo, z_buf, True)
 
     def store_filter(j, rows, lanes, y):
         gf_ref[pl.ds(rows, row_step), pl.ds(pl.multiple_of(j * tok + lanes, lane_step), lane_step)] = y
 
     inverse_outer(store_filter)
 
-    wait_all(conv_t, 6)
-
-    def output_step(i, carry):
-        cols = pl.ds(pl.multiple_of(i * group, group), group)
-        conv = conv_t[cols, :].astype(F32).T
-        out_ref[:, cols] = (q_seq[:, cols].astype(F32) * conv).astype(BF)
-        gq_ref[:, cols] = (gtok[:, cols].astype(F32) * conv).astype(BF)
-        return carry
-
-    lax.fori_loop(0, side, output_step, 0)
-
-    wait_all(gs_t, 7)
-
-    def gradient_step(i, carry):
-        cols = pl.ds(pl.multiple_of(i * group, group), group)
-        grad = gs_t[cols, :].astype(F32).T
-        gk_ref[:, cols] = (grad * v_seq[:, cols].astype(F32)).astype(BF)
-        gv_ref[:, cols] = (grad * k_seq[:, cols].astype(F32)).astype(BF)
-        return carry
-
-    lax.fori_loop(0, side, gradient_step, 0)
+    hand_out(gf_ref, f_out, 4)
+
+    wait_all(conv_o, 6)
+    wait_all(gs_o, 7)
+    for n, (src, dst) in enumerate(
+        ((k_seq, k_out), (v_seq, v_out), (q_seq, q_out), (gtok, g_out), (gf_ref, f_out))
+    ):
+        pltpu.make_async_copy(src, dst, out_sem.at[n]).wait()
 
     def wait_sent(buf, n):
         pltpu.make_async_copy(buf, buf, send_sem.at[n]).wait()
@@ -434,6 +432,34 @@
     wait_sent(gc_in.at[parts_sent], 5)
     wait_sent(conv_o.at[parts_sent], 6)
     wait_sent(gs_o.at[parts_sent], 7)
+
+
+def finish_body(q, g, k, v, conv_t, gs_t, f_in, out, gq, gk, gv, f_out):
+    conv = conv_t[...].astype(F32).T
+    out[...] = (q[...].astype(F32) * conv).astype(BF)
+    gq[...] = (g[...].astype(F32) * conv).astype(BF)
+    grad = gs_t[...].astype(F32).T
+    gk[...] = (grad * v[...].astype(F32)).astype(BF)
+    gv[...] = (grad * k[...].astype(F32)).astype(BF)
+    f_out[...] = f_in[...]
+
+
+def finish(q, g, k, v, conv_t, gs_t, grad_filters):
+    tok, width = q.shape
+    chan, lags = grad_filters.shape
+    steps = 4
+    seq = pl.BlockSpec((tok, width // steps), lambda i: (0, i))
+    seq_t = pl.BlockSpec((width // steps, tok), lambda i: (i, 0))
+    filt = pl.BlockSpec((chan // steps, lags), lambda i: (i, 0))
+    seq_out = jax.ShapeDtypeStruct((tok, width), BF)
+    return pl.pallas_call(
+        finish_body,
+        grid=(steps,),
+        out_shape=(seq_out,) * 4 + (jax.ShapeDtypeStruct((chan, lags), F32),),
+        in_specs=[seq] * 4 + [seq_t] * 2 + [filt],
+        out_specs=(seq,) * 4 + (filt,),
+        compiler_params=pltpu.CompilerParams(vmem_limit_bytes=58 * 1024 * 1024),
+    )(q, g, k, v, conv_t, gs_t, grad_filters)
 
 
 def solution(mesh):
@@ -463,28 +489,32 @@
         def body(*refs):
             kernel_body((n_ctx, n_tp, tok, slot, chan), *refs)
 
-        return pl.pallas_call(
+        seq_t_out = jax.ShapeDtypeStruct((width, tok), BF)
+
+        parts_out = pl.pallas_call(
             body,
-            out_shape=(seq_out, seq_out, seq_out, seq_out, jax.ShapeDtypeStruct(filters.shape, F32)),
+            out_shape=(seq_out,) * 4 + (seq_t_out,) * 2 + (jax.ShapeDtypeStruct(filters.shape, F32),),
             in_specs=[any_spec] * 9 + [vmem_spec] * 4,
-            out_specs=(vmem_spec,) * 5,
+            out_specs=(any_spec,) * 7,
             scratch_shapes=[
                 rows_bf, rows_bf, rows_bf, seq, vm(filters.shape, F32), table, table, table, table,
                 vm((tok, n_ctx * slot), BF), seq, seq, seq, seq_t, seq_t, parts, parts,
                 half_spec, half_spec, spec, spec, spec, spec,
-                parts, parts, seq_t, seq_t,
+                parts, parts, vm(filters.shape, F32),
                 pltpu.SemaphoreType.DMA((8,)),
                 pltpu.SemaphoreType.DMA((8,)),
                 pltpu.SemaphoreType.DMA((5,)),
+                pltpu.SemaphoreType.DMA((5,)),
             ],
             compiler_params=pltpu.CompilerParams(
-                collective_id=0, has_side_effects=True, vmem_limit_bytes=56 * 1024 * 1024
+                collective_id=0, has_side_effects=True, vmem_limit_bytes=58 * 1024 * 1024
             ),
         )(
             query_rows, key_rows, value_rows, grad_out, filters,
             wf_hi, wf_lo, wi_hi, wi_lo,
             own, bias_term.reshape(chan, 1), cos, sin,
         )
+        return finish(*parts_out)
 
     in_specs = (
         P("ctx", "tp"),

time: 91.2 us -> 79.6 us (0.87)
  local copies, waits for them, and re-layouts: 7.92 us -> 2.19 us
  Pallas kernels: 81.6 us -> 76.2 us
    unnamed x17 -> x4, local copies, waits for them, and re-layouts: 6.48 us -> 0.76 us
    pallas_call x1 -> x2, Pallas kernels: 81.6 us -> 76.2 us  [the longest x1 71.6 us: per_device(): pl.pallas_call(body, out_shape=(seq_out,) * 4 + (seq_t_out,) * 2 + (jax.S...]
where the time goes in v1:
time: 79.6 us; the launch traced here: 79.1 us
  Pallas kernels  76.2 us (96%)
  local copies, waits for them, and re-layouts  2.19 us (3%)
    pallas_call x1, Pallas kernels, per_device(): pl.pallas_call(body, out_shape=(seq_out,) * 4 + (seq_t_out,) * 2 + (jax.S...  71.6 us
    pallas_call x1, Pallas kernels, finish(): pl.pallas_call(finish_body, grid=(steps,), out_shape=(seq_out,) * 4 + (ja...  4.61 us

profile of v1, /device:TPU:2, one launch (start us, length us, event | category | flops | bytes accessed | tf_op | source)
XLA Modules:
  0.0 79.1 jit_solution(11937260094833035819)
XLA Ops:
  0.6 0.0 copy-start
  0.7 0.7 copy-done
  1.4 0.1 constant_dynamic-slice_fusion
  1.5 0.0 copy-start.1
  1.5 0.7 reshape.16.refs_9_
  2.1 0.0 copy-done.1
  2.1 0.7 copy.18.refs_10_
  2.8 71.6 %shard_map.164 = (bf16[256,1024]{1,0:T(8,128)(2,1)}, bf16[256,1024]{1,0:T(8,128)(2,1)}, bf16[256,1024]{1,0:T(8,128)(2,1)}, bf16[256,1024]{1,0:T(8,128)(2,1)}, bf...) custom-call(bf16[512,1024]{1,0:T(8,128)(2,1)} %refs_0_.1, bf16[512,1024]{1,0:T(8,128)(2,1)} %refs_1_.1, ...), custom_call_target="tpu_custom_call" | custom-call | tf_op jit(solution)/shard_map/pallas_call | solution.py:494
  74.5 4.6 %shard_map.165 = (bf16[256,1024]{1,0:T(8,128)(2,1)}, bf16[256,1024]{1,0:T(8,128)(2,1)}, bf16[256,1024]{1,0:T(8,128)(2,1)}, bf16[256,1024]{1,0:T(8,128)(2,1)}, f32[64,4096]{1,0:T(8,128)}) custom-call(bf16[256,1024]{1,0:T(8,128)(2,1)} %get-tuple-element.12.q, bf16[256,1024]{1,0:T(8,128)(2,1)} %get-tuple-element.13.g, bf16[256,1024]{1,0:T(8,128)(2,1)} %get-tuple-element.14.k, ...), custom_call_target="tpu_custom_call" | custom-call | tf_op jit(solution)/shard_map/pallas_call | solution.py:455
Async XLA Ops:
  0.6 0.8 copy-start
  1.5 0.7 copy-start.1

commit v2 on v1

--- a/solution.py
+++ b/solution.py
@@ -91,12 +91,12 @@
 def kernel_body(
     sizes,
     q_hbm, k_hbm, v_hbm, g_hbm, f_hbm, wf_hi_hbm, wf_lo_hbm, wi_hi_hbm, wi_lo_hbm,
-    slot_ref, bias_ref, cos_ref, sin_ref,
+    positions_ref, bias_row, cos_ref, sin_ref,
     q_out, g_out, k_out, v_out, conv_t, gs_t, f_out,
     rq, rk, rv, gtok, f_buf, wf_hi, wf_lo, wi_hi, wi_lo,
     hot, q_seq, k_seq, v_seq, sig_t, gc_t, sig_in, gc_in,
     l_hi, l_lo, spec_f, spec_s, spec_g, z_buf,
-    conv_o, gs_o, gf_ref,
+    conv_o, gs_o, gf_ref, bias_ref,
     recv_sem, send_sem, local_sem, out_sem,
 ):
     n_ctx, n_tp, tok, slot, chan = sizes
@@ -180,8 +180,19 @@
     lax.fori_loop(1, n_tp, send_grad, 0)
     send_rows(q_hbm, rq, 2)
 
+    rows_all = n_ctx * slot
+    lane = lax.broadcasted_iota(jnp.int32, (rows_all, rows_all), 1)
+    column = lax.broadcasted_iota(jnp.int32, (rows_all, rows_all), 0)
+    pick = jnp.where(column == me * slot + lane % slot, 1.0, 0.0).astype(BF)
+    mine = jnp.dot(
+        positions_ref[...].astype(F32).astype(BF), pick, preferred_element_type=F32
+    )
+    buffer = lax.broadcasted_iota(jnp.int32, mine.shape, 0)
+    keep = lax.broadcasted_iota(jnp.int32, mine.shape, 1) // slot == buffer
+    slots = jnp.sum(jnp.where(keep, mine, 0.0), axis=0, keepdims=True).astype(jnp.int32)
+    bias_ref[...] = jnp.broadcast_to(bias_row[...], (128, chan)).T
     hot[...] = jnp.where(
-        slot_ref[...] == lax.broadcasted_iota(jnp.int32, hot.shape, 0), 1.0, 0.0
+        slots == lax.broadcasted_iota(jnp.int32, hot.shape, 0), 1.0, 0.0
     ).astype(BF)
 
     row_step, lane_step = 16, 128
@@ -230,8 +241,8 @@
             at = pl.ds(pl.multiple_of(m * block_rows, row_step), block_rows)
             a = l_hi[at, :]
             total = jnp.dot(a, high[...], preferred_element_type=F32)
-            total += jnp.dot(a, low[...], preferred_element_type=F32)
             if exact:
+                total += jnp.dot(a, low[...], preferred_element_type=F32)
                 total += jnp.dot(l_lo[at, :], high[...], preferred_element_type=F32)
             dest[at, :] = total
             return carry
@@ -301,7 +312,7 @@
     group = side * chan
 
     def send_channels(src, dst, n, y):
-        def one(dx, carry):
+        for dx in (2, 1, 3, 0):
             d = y * side + (my_x + dx) % side
             at = pl.ds(pl.multiple_of(d * chan, chan), chan)
             pl.when(d != me)(
@@ -314,9 +325,6 @@
                     device_id_type=MESH,
                 ).start()
             )
-            return carry
-
-        lax.fori_loop(0, side, one, 0)
 
     def send_own_channels(src, dst, n):
         at = pl.ds(pl.multiple_of(me * chan, chan), chan)
@@ -326,7 +334,7 @@
     wait_all(rv, 1)
 
     def signal_step(i, carry):
-        y = (my_y + i) % side
+        y = (my_y + i + 1) % side
         cols = pl.ds(pl.multiple_of(y * group, group), group)
         key = settled(rk, cols)
         value = settled(rv, cols)
@@ -345,7 +353,7 @@
     wait_all(gtok, 3)
 
     def grad_step(i, carry):
-        y = (my_y + i) % side
+        y = (my_y + i + 1) % side
         cols = pl.ds(pl.multiple_of(y * group, group), group)
         query = settled(rq, cols)
         q_seq[:, cols] = query.astype(BF)
@@ -471,8 +479,6 @@
         tok = grad_out.shape[0] * n_tp
         chan = filters.shape[0]
         (wf_hi, wf_lo), (wi_hi, wi_lo), cos, sin = make_tables(n_ctx, tok)
-        own = lax.dynamic_slice_in_dim(positions, lax.axis_index("ctx") * slot, slot, 1)
-        own = own.reshape(1, n_ctx * slot)
         bins = n_ctx + 1
         vm = pltpu.VMEM
         rows_bf = vm((n_ctx * slot, width), BF)
@@ -500,7 +506,7 @@
                 rows_bf, rows_bf, rows_bf, seq, vm(filters.shape, F32), table, table, table, table,
                 vm((tok, n_ctx * slot), BF), seq, seq, seq, seq_t, seq_t, parts, parts,
                 half_spec, half_spec, spec, spec, spec, spec,
-                parts, parts, vm(filters.shape, F32),
+                parts, parts, vm(filters.shape, F32), vm((chan, 128), F32),
                 pltpu.SemaphoreType.DMA((8,)),
                 pltpu.SemaphoreType.DMA((8,)),
                 pltpu.SemaphoreType.DMA((5,)),
@@ -512,7 +518,7 @@
         )(
             query_rows, key_rows, value_rows, grad_out, filters,
             wf_hi, wf_lo, wi_hi, wi_lo,
-            own, bias_term.reshape(chan, 1), cos, sin,
+            positions, bias_term.reshape(1, chan), cos, sin,
         )
         return finish(*parts_out)
 

time: 79.6 us -> 76.4 us (0.960)
  local copies, waits for them, and re-layouts: 2.19 us -> 0 us
    reshape x2 -> x0, local copies, waits for them, and re-layouts: 1.37 us -> none  [the longest x1 0.71 us: per_device(): bias_term.reshape(chan, 1)]
where the time goes in v2:
time: 76.4 us; the launch traced here: 76.1 us
  Pallas kernels  75.5 us (99%)
    pallas_call x1, Pallas kernels, per_device(): pl.pallas_call(body, out_shape=(seq_out,) * 4 + (seq_t_out,) * 2 + (jax.S...  70.9 us
    pallas_call x1, Pallas kernels, finish(): pl.pallas_call(finish_body, grid=(steps,), out_shape=(seq_out,) * 4 + (ja...  4.61 us

profile of v2, /device:TPU:2, one launch (start us, length us, event | category | flops | bytes accessed | tf_op | source)
XLA Modules:
  0.0 76.1 jit_solution(7234774400764536497)
XLA Ops:
  0.6 70.9 %shard_map.164 = (bf16[256,1024]{1,0:T(8,128)(2,1)}, bf16[256,1024]{1,0:T(8,128)(2,1)}, bf16[256,1024]{1,0:T(8,128)(2,1)}, bf16[256,1024]{1,0:T(8,128)(2,1)}, bf...) custom-call(bf16[512,1024]{1,0:T(8,128)(2,1)} %refs_0_.1, bf16[512,1024]{1,0:T(8,128)(2,1)} %refs_1_.1, ...), custom_call_target="tpu_custom_call" | custom-call | tf_op jit(solution)/shard_map/pallas_call | solution.py:500
  71.5 4.6 %shard_map.165 = (bf16[256,1024]{1,0:T(8,128)(2,1)}, bf16[256,1024]{1,0:T(8,128)(2,1)}, bf16[256,1024]{1,0:T(8,128)(2,1)}, bf16[256,1024]{1,0:T(8,128)(2,1)}, f32[64,4096]{1,0:T(8,128)}) custom-call(bf16[256,1024]{1,0:T(8,128)(2,1)} %get-tuple-element.12.q, bf16[256,1024]{1,0:T(8,128)(2,1)} %get-tuple-element.13.g, bf16[256,1024]{1,0:T(8,128)(2,1)} %get-tuple-element.14.k, ...), custom_call_target="tpu_custom_call" | custom-call | tf_op jit(solution)/shard_map/pallas_call | solution.py:463

commit v3 on v2

--- a/solution.py
+++ b/solution.py
@@ -267,7 +267,7 @@
 
         lax.fori_loop(0, total_rows // row_step, step, 0)
 
-    def inverse_outer(store):
+    def inverse_outer(store, middle=None):
         def step(it, carry):
             rows, lanes = place(it)
             spectrum = []
@@ -288,7 +288,10 @@
                 store(j, rows, lanes, y * (factor * inv_len))
             return carry
 
-        lax.fori_loop(0, pieces, step, 0)
+        lax.fori_loop(0, pieces // 2, step, 0)
+        if middle is not None:
+            middle()
+        lax.fori_loop(pieces // 2, pieces, step, 0)
 
     for copy in loads:
         copy.wait()
@@ -366,12 +369,15 @@
     hand_out(q_seq, q_out, 2)
     hand_out(gtok, g_out, 3)
 
-    def send_tokens(src, dst, n):
-        at = pl.ds(pl.multiple_of(me * chan, chan), chan)
+    half_chan = chan // 2
+
+    def send_tokens(src, dst, n, part):
+        from_rows = pl.ds(part * half_chan, half_chan)
+        at = pl.ds(pl.multiple_of(me * chan + part * half_chan, half_chan), half_chan)
 
         def one(d):
             pltpu.make_async_remote_copy(
-                src_ref=src.at[d],
+                src_ref=src.at[d, from_rows, :],
                 dst_ref=dst.at[at, :],
                 send_sem=send_sem.at[n],
                 recv_sem=recv_sem.at[n],
@@ -379,7 +385,7 @@
                 device_id_type=MESH,
             ).start()
 
-        pltpu.make_async_copy(src.at[me], dst.at[at, :], recv_sem.at[n]).start()
+        pltpu.make_async_copy(src.at[me, from_rows, :], dst.at[at, :], recv_sem.at[n]).start()
         each_partner(one)
 
     def piece(buf, j, rows, lanes):
@@ -399,16 +405,16 @@
     inner(wf_hi, wf_lo, spec_s, False)
     multiply(spec_f, spec_s, False, False)
     inner(wi_hi, wi_lo, z_buf, False)
-    inverse_outer(store_with_bias(sig_in, conv_o))
-    send_tokens(conv_o, conv_t, 6)
+    inverse_outer(store_with_bias(sig_in, conv_o), lambda: send_tokens(conv_o, conv_t, 6, 0))
+    send_tokens(conv_o, conv_t, 6, 1)
 
     wait_all(gc_in, 5)
     forward_outer(lambda j, rows, lanes: piece(gc_in, j, rows, lanes), False)
     inner(wf_hi, wf_lo, spec_g, False)
     multiply(spec_f, spec_g, True, False)
     inner(wi_hi, wi_lo, z_buf, False)
-    inverse_outer(store_with_bias(gc_in, gs_o))
-    send_tokens(gs_o, gs_t, 7)
+    inverse_outer(store_with_bias(gc_in, gs_o), lambda: send_tokens(gs_o, gs_t, 7, 0))
+    send_tokens(gs_o, gs_t, 7, 1)
 
     multiply(spec_s, spec_g, True, True)
     inner(wi_hi, wi_lo, z_buf, True)
@@ -455,7 +461,7 @@
 def finish(q, g, k, v, conv_t, gs_t, grad_filters):
     tok, width = q.shape
     chan, lags = grad_filters.shape
-    steps = 4
+    steps = 2
     seq = pl.BlockSpec((tok, width // steps), lambda i: (0, i))
     seq_t = pl.BlockSpec((width // steps, tok), lambda i: (i, 0))
     filt = pl.BlockSpec((chan // steps, lags), lambda i: (i, 0))

time: 76.4 us -> 74.8 us (0.979)
  Pallas kernels: 75.5 us -> 73.9 us
    pallas_call x1, Pallas kernels: 4.61 us -> 3.51 us  [finish(): pl.pallas_call(finish_body, grid=(steps,), out_shape=(seq_out,) * 4 + (ja...]
where the time goes in v3:
time: 74.8 us; the launch traced here: 74.6 us
  Pallas kernels  73.9 us (99%)
    pallas_call x1, Pallas kernels, per_device(): pl.pallas_call(body, out_shape=(seq_out,) * 4 + (seq_t_out,) * 2 + (jax.S...  70.4 us
    pallas_call x1, Pallas kernels, finish(): pl.pallas_call(finish_body, grid=(steps,), out_shape=(seq_out,) * 4 + (ja...  3.51 us

profile of v3, /device:TPU:2, one launch (start us, length us, event | category | flops | bytes accessed | tf_op | source)
XLA Modules:
  0.0 74.6 jit_solution(8058898332796950279)
XLA Ops:
  0.6 70.4 %shard_map.164 = (bf16[256,1024]{1,0:T(8,128)(2,1)}, bf16[256,1024]{1,0:T(8,128)(2,1)}, bf16[256,1024]{1,0:T(8,128)(2,1)}, bf16[256,1024]{1,0:T(8,128)(2,1)}, bf...) custom-call(bf16[512,1024]{1,0:T(8,128)(2,1)} %refs_0_.1, bf16[512,1024]{1,0:T(8,128)(2,1)} %refs_1_.1, ...), custom_call_target="tpu_custom_call" | custom-call | tf_op jit(solution)/shard_map/pallas_call | solution.py:506
  71.1 3.5 %shard_map.165 = (bf16[256,1024]{1,0:T(8,128)(2,1)}, bf16[256,1024]{1,0:T(8,128)(2,1)}, bf16[256,1024]{1,0:T(8,128)(2,1)}, bf16[256,1024]{1,0:T(8,128)(2,1)}, f32[64,4096]{1,0:T(8,128)}) custom-call(bf16[256,1024]{1,0:T(8,128)(2,1)} %get-tuple-element.12.q, bf16[256,1024]{1,0:T(8,128)(2,1)} %get-tuple-element.13.g, bf16[256,1024]{1,0:T(8,128)(2,1)} %get-tuple-element.14.k, ...), custom_call_target="tpu_custom_call" | custom-call | tf_op jit(solution)/shard_map/pallas_call | solution.py:469

commit v4 on v3

--- a/solution.py
+++ b/solution.py
@@ -267,6 +267,22 @@
 
         lax.fori_loop(0, total_rows // row_step, step, 0)
 
+    def product_inner(one, two, conjugate_one):
+        def step(m, carry):
+            at = pl.ds(pl.multiple_of(m * block_rows, row_step), block_rows)
+            a, b = one[at, :tok], one[at, tok:]
+            c, d = two[at, :tok], two[at, tok:]
+            if conjugate_one:
+                re, im = a * c + b * d, a * d - b * c
+            else:
+                re, im = a * c - b * d, a * d + b * c
+            z_buf[at, :] = jnp.dot(
+                re.astype(BF), wi_hi[:tok, :], preferred_element_type=F32
+            ) + jnp.dot(im.astype(BF), wi_hi[tok:, :], preferred_element_type=F32)
+            return carry
+
+        lax.fori_loop(0, 4, step, 0)
+
     def inverse_outer(store, middle=None):
         def step(it, carry):
             rows, lanes = place(it)
@@ -403,16 +419,14 @@
     wait_all(sig_in, 4)
     forward_outer(lambda j, rows, lanes: piece(sig_in, j, rows, lanes), False)
     inner(wf_hi, wf_lo, spec_s, False)
-    multiply(spec_f, spec_s, False, False)
-    inner(wi_hi, wi_lo, z_buf, False)
+    product_inner(spec_f, spec_s, False)
     inverse_outer(store_with_bias(sig_in, conv_o), lambda: send_tokens(conv_o, conv_t, 6, 0))
     send_tokens(conv_o, conv_t, 6, 1)
 
     wait_all(gc_in, 5)
     forward_outer(lambda j, rows, lanes: piece(gc_in, j, rows, lanes), False)
     inner(wf_hi, wf_lo, spec_g, False)
-    multiply(spec_f, spec_g, True, False)
-    inner(wi_hi, wi_lo, z_buf, False)
+    product_inner(spec_f, spec_g, True)
     inverse_outer(store_with_bias(gc_in, gs_o), lambda: send_tokens(gs_o, gs_t, 7, 0))
     send_tokens(gs_o, gs_t, 7, 1)
 

time: 74.8 us -> 74.1 us (level)
  no operation moved by 1% of the time
where the time goes in v4:
time: 74.1 us; the launch traced here: 73.9 us
  Pallas kernels  73.3 us (99%)
    pallas_call x1, Pallas kernels, per_device(): pl.pallas_call(body, out_shape=(seq_out,) * 4 + (seq_t_out,) * 2 + (jax.S...  69.8 us
    pallas_call x1, Pallas kernels, finish(): pl.pallas_call(finish_body, grid=(steps,), out_shape=(seq_out,) * 4 + (ja...  3.51 us

profile of v4, /device:TPU:2, one launch (start us, length us, event | category | flops | bytes accessed | tf_op | source)
XLA Modules:
  0.0 73.9 jit_solution(8840504193958039859)
XLA Ops:
  0.6 69.8 %shard_map.164 = (bf16[256,1024]{1,0:T(8,128)(2,1)}, bf16[256,1024]{1,0:T(8,128)(2,1)}, bf16[256,1024]{1,0:T(8,128)(2,1)}, bf16[256,1024]{1,0:T(8,128)(2,1)}, bf...) custom-call(bf16[512,1024]{1,0:T(8,128)(2,1)} %refs_0_.1, bf16[512,1024]{1,0:T(8,128)(2,1)} %refs_1_.1, ...), custom_call_target="tpu_custom_call" | custom-call | tf_op jit(solution)/shard_map/pallas_call | solution.py:520
  70.4 3.5 %shard_map.165 = (bf16[256,1024]{1,0:T(8,128)(2,1)}, bf16[256,1024]{1,0:T(8,128)(2,1)}, bf16[256,1024]{1,0:T(8,128)(2,1)}, bf16[256,1024]{1,0:T(8,128)(2,1)}, f32[64,4096]{1,0:T(8,128)}) custom-call(bf16[256,1024]{1,0:T(8,128)(2,1)} %get-tuple-element.12.q, bf16[256,1024]{1,0:T(8,128)(2,1)} %get-tuple-element.13.g, bf16[256,1024]{1,0:T(8,128)(2,1)} %get-tuple-element.14.k, ...), custom_call_target="tpu_custom_call" | custom-call | tf_op jit(solution)/shard_map/pallas_call | solution.py:483
